TPU v7x, 32 devices: a whole 2x2x4 slice. The times are simulated.
32 devices in a mesh: dp: 2 (over y), expert: 16 (over z, x, core).
Axes of the slice: x: 2, y: 2, z: 4, core: 2. Of those that a mesh axis runs over, the one named last changes fastest.
Arguments:
- cache: bfloat16 [4, 64, 1152], P('dp'), may hold values from -6 to 6
- requests: int32 [2, 16, 2], P(None, 'expert'), may hold values from 0 to 3
- routes: int32 [4096, 1], P('expert'), may hold values from 0 to 15; in each aligned block of 256 rows (0 to 255, 256 to 511, ...) at most 20 rows name the same one
- combine_weight: float32 [4096, 1], P('expert'), may hold values from 0.2 to 1
- proj_weight: bfloat16 [1152, 2048], P('expert', 'dp'), may hold values from -1 to 1
- norm_gain: float32 [2048], replicated, may hold values from 0.5 to 1.5
- gate_weight: bfloat16 [16, 2048, 1408], P('expert', None, 'dp'), may hold values from -0.125 to 0.125
- up_weight: bfloat16 [16, 2048, 1408], P('expert', None, 'dp'), may hold values from -0.125 to 0.125
- down_weight: bfloat16 [16, 1408, 2048], P('expert', None, 'dp'), may hold values from -0.15625 to 0.15625
- cotangent: bfloat16 [4096, 2048], P('expert', 'dp'), may hold values from -6 to 6
Outputs:
- mixed: bfloat16 [4096, 2048], P('expert', 'dp')
- down_grad: bfloat16 [16, 1408, 2048], P('expert', None, 'dp')
Inputs may be any that keep to these rules, and one draw needn't show every extreme that they name: `routes`: among the 256 tokens of one column no expert is named more than 20 times, and in every draw some column names some expert exactly 20 times.
All inputs are finite; a program needn't handle non-finite values.
Results may differ from a plain program's by a relative error of at most 0.012.
Values may be sent and summed in bfloat16 or wider, within the bound.
A program may use at most 64 MiB of HBM per device.

v0:
```python
import jax
import jax.numpy as jnp
from jax import lax
from jax.sharding import PartitionSpec as P


def normalize(row_block, gain_row, sum_squares, model_width):
    inv_scale = lax.rsqrt(sum_squares / model_width + 1e-06)
    return (row_block.astype(jnp.float32) * inv_scale[:, None] * gain_row[None, :]).astype(
        jnp.bfloat16
    )


def local_squares(row_block):
    values = row_block.astype(jnp.float32)
    return jnp.sum(values * values, axis=1)


def body(
    cache,
    requests,
    routes,
    combine_weight,
    proj_weight,
    norm_gain,
    gate_weight,
    up_weight,
    down_weight,
    cotangent,
):
    dp_rank = lax.axis_index("dp")
    model_width = norm_gain.shape[0]
    slice_width = cotangent.shape[1]
    wanted = requests.reshape(-1)
    request_count = wanted.shape[0]
    shard_piece = lax.all_gather(cache, "dp", axis=0, tiled=True)
    matches = (wanted[:, None] == jnp.arange(shard_piece.shape[0])[None, :]).astype(jnp.bfloat16)
    matched = jnp.einsum("rk,kpf->rpf", matches, shard_piece, preferred_element_type=jnp.float32)
    fetched = matched.astype(jnp.bfloat16)
    features = fetched.reshape(request_count * cache.shape[1], cache.shape[2])
    tokens = features.shape[0]
    projected = jnp.dot(
        features,
        lax.all_gather(proj_weight, "expert", axis=0, tiled=True),
        preferred_element_type=jnp.float32,
    ).astype(jnp.bfloat16)
    gain_slice = lax.dynamic_slice_in_dim(norm_gain, dp_rank * slice_width, slice_width)
    sum_squares = lax.psum(local_squares(projected), "dp")
    source_rows = normalize(projected, gain_slice, sum_squares, model_width)
    experts = lax.axis_size("expert") * gate_weight.shape[0]
    capacity = max(2, 5 * tokens // (4 * experts))
    expert_id = routes[:, 0]
    onehot = (expert_id[:, None] == jnp.arange(experts, dtype=jnp.int32)[None, :]).astype(jnp.int32)
    slot_rank = jnp.sum((jnp.cumsum(onehot, axis=0) - 1) * onehot, axis=1)
    position = expert_id * capacity + slot_rank
    slot_map = (
        jnp.zeros((experts * capacity,), jnp.int32)
        .at[position]
        .set(jnp.arange(tokens, dtype=jnp.int32) + 1)
    )
    filled = slot_map > 0
    source_row = jnp.maximum(slot_map - 1, 0)

    def arrange(row_block):
        picked = jnp.where(filled[:, None], row_block[source_row], jnp.zeros((), row_block.dtype))
        return picked.reshape(experts, capacity, row_block.shape[1])

    token_weight = combine_weight[:, 0]
    scaled_grad = (token_weight[:, None] * cotangent.astype(jnp.float32)).astype(jnp.bfloat16)
    sent_rows, sent_grad = (
        lax.all_to_all(arrange(source_rows), "expert", split_axis=0, concat_axis=0, tiled=True),
        lax.all_to_all(arrange(scaled_grad), "expert", split_axis=0, concat_axis=0, tiled=True),
    )
    slot_count = sent_rows.shape[0] * sent_rows.shape[1]
    full_rows = lax.all_gather(sent_rows.reshape(slot_count, slice_width), "dp", axis=1, tiled=True)
    grad_rows = sent_grad.reshape(slot_count, slice_width)
    gate_act = jnp.dot(full_rows, gate_weight[0], preferred_element_type=jnp.float32)
    up_act = jnp.dot(full_rows, up_weight[0], preferred_element_type=jnp.float32)
    hidden = (jax.nn.silu(gate_act) * up_act).astype(jnp.bfloat16)
    down_local = down_weight[0]
    shard_piece = lax.all_gather(hidden, "dp", axis=1, tiled=True)
    out_sum = jnp.dot(shard_piece, down_local, preferred_element_type=jnp.float32)
    grad_block = lax.dot_general(
        shard_piece, grad_rows, (((0,), (0,)), ((), ())), preferred_element_type=jnp.float32
    )
    grad_sum = grad_block
    out_sum, grad_sum = (out_sum, grad_sum)
    expert_out = out_sum.astype(jnp.bfloat16).reshape(sent_rows.shape[0], capacity, slice_width)
    returned = lax.all_to_all(expert_out, "expert", split_axis=0, concat_axis=0, tiled=True)
    returned_flat = returned.reshape(experts * capacity, slice_width)
    mixed_out = (token_weight[:, None] * returned_flat[position].astype(jnp.float32)).astype(
        jnp.bfloat16
    )
    return (mixed_out, grad_sum.astype(jnp.bfloat16)[None])


def solution(mesh):
    return jax.shard_map(
        body,
        mesh=mesh,
        in_specs=(
            P("dp", None, None),
            P(None, "expert", None),
            P("expert", None),
            P("expert", None),
            P("expert", "dp"),
            P(),
            P("expert", None, "dp"),
            P("expert", None, "dp"),
            P("expert", None, "dp"),
            P("expert", "dp"),
        ),
        out_specs=(P("expert", "dp"), P("expert", None, "dp")),
        check_vma=False,
    )
```

profile of v0, /device:TPU:9, one launch (start us, length us, event | category | flops | bytes accessed | tf_op | source)
XLA Modules:
  0.0 185.4 jit_solution(7512770705820136966)
XLA Ops:
  8.5 1.3 reduce.5
  9.9 8.8 %all_gather.12 = bf16[4,64,1152]{2,1,0:T(8,128)(2,1)S(1)} all-gather(bf16[2,64,1152]{2,1,0:T(8,128)(2,1)} %param.10), channel_id=1, replica_groups=mesh['dp'=2,'expert'=16] {'dp'}, dimensions={0}, use_global_device_ids=true | all-gather | bytes 884736 | tf_op jit(solution)/shard_map/all_gather | solution.py:36
  19.3 0.9 copy.19
  21.1 1.4 scatter_custom_fusion
  22.5 1.2 multiply_convert_fusion
  23.7 2.6 %gather_fusion.2 = bf16[320,1024]{1,0:T(8,128)(2,1)} fusion(bf16[256,1024]{1,0:T(8,128)(2,1)S(1)} %multiply_convert_fusion, s32[1024]{0:T(1024)S(1)} %pad_clamp_fusion.1), kind=kCustom, calls=%fused_computation.2 | custom fusion | bytes 1312000 | tf_op jit(solution)/shard_map/gather | solution.py:65
  26.4 2.0 %gather.17 = bf16[16,20,1024]{2,1,0:T(8,128)(2,1)} reshape(bf16[320,1024]{1,0:T(8,128)(2,1)} %gather_fusion.2) | data formatting | bytes 1310720 | tf_op jit(solution)/shard_map/gather | solution.py:65
  28.5 25.1 %all-gather.4.cloned.1.call-done = bf16[1152,1024]{1,0:T(8,128)(2,1)} async-done(((bf16[72,1024]{1,0:T(8,128)(2,1)}), bf16[1152,1024]{1,0:T(8,128)(2,1)}) %all-gather.4.cloned.1.call-update) | async-done | bytes 2359312 | tf_op jit(solution)/shard_map/all_gather | solution.py:44
  53.6 3.5 %fusion.19 = (f32[256]{0:T(256)S(1)}, bf16[256,1024]{1,0:T(8,128)(2,1)}) fusion(bf16[256,1152]{1,0:T(8,128)(2,1)} %bitcast.56, bf16[1152,1024]{1,0:T(8,128)(2,1)} %all-gather.4.cloned.1.call-done), kind=kOutput, calls=%fused_computation.20 | convolution fusion | flops 605028096 | bytes 3474432 | tf_op jit(solution)/shard_map/dot_general | solution.py:42
  57.1 3.8 %psum.7 = f32[256]{0:T(256)S(1)} all-reduce(f32[256]{0:T(256)S(1)} %get-tuple-element.4), channel_id=1, replica_groups=mesh['dp'=2,'expert'=16] {'dp'}, use_global_device_ids=true, to_apply=%region_5.6 | all-reduce | flops 256 | bytes 2048 | tf_op jit(solution)/shard_map/psum | solution.py:48
  60.9 1.2 fusion.21
  62.1 2.6 %gather_fusion = bf16[320,1024]{1,0:T(8,128)(2,1)} fusion(bf16[256,1024]{1,0:T(8,128)(2,1)S(1)} %fusion.21, s32[1024]{0:T(1024)S(1)} %pad_clamp_fusion.1), kind=kCustom, calls=%fused_computation | custom fusion | bytes 1312000 | tf_op jit(solution)/shard_map/gather | solution.py:65
  64.8 2.0 %gather.14 = bf16[16,20,1024]{2,1,0:T(8,128)(2,1)} reshape(bf16[320,1024]{1,0:T(8,128)(2,1)} %gather_fusion) | data formatting | bytes 1310720 | tf_op jit(solution)/shard_map/gather | solution.py:65
  66.8 2.4 %broadcast_select_fusion = (bf16[16,20,1024]{2,1,0:T(8,128)(2,1)}, bf16[16,20,1024]{2,1,0:T(8,128)(2,1)S(1)}) fusion(bf16[16,20,1024]{2,1,0:T(8,128)(2,1)} %gather.17, pred[16,20]{1,0:T(8,128)(4,1)S(1)} %broadcast_in_dim.33, bf16[16,20,1024]{2,1,0:T(8,128)(2,1)} %gather.14), kind=kLoop, calls=%fused_computation.25 | loop fusion | flops 655360 | bytes 2621760 | tf_op jit(solution)/shard_map/jit(_where)/select_n | solution.py:65
  69.2 25.4 %all_to_all.15 = bf16[16,20,1024]{2,1,0:T(8,128)(2,1)} all-to-all(bf16[16,20,1024]{2,1,0:T(8,128)(2,1)S(1)} %get-tuple-element.3), channel_id=1, replica_groups=mesh['dp'=2,'expert'=16] {'expert'}, dimensions={0} | all-to-all | bytes 1310720 | tf_op jit(solution)/shard_map/all_to_all | solution.py:71
  94.6 2.0 %reshape.57 = bf16[320,1024]{1,0:T(8,128)(2,1)} reshape(bf16[16,20,1024]{2,1,0:T(8,128)(2,1)} %all_to_all.15) | data formatting | bytes 1310720 | tf_op jit(solution)/shard_map/reshape | solution.py:75
  96.6 4.5 %all-to-all-start.2 = ((bf16[16,20,1024]{2,1,0:T(8,128)(2,1)}), bf16[16,20,1024]{2,1,0:T(8,128)(2,1)}, u32[]{:S(2)}, u32[]{:S(2)}) async-start(bf16[16,20,1024]{2,1,0:T(8,128)(2,1)} %get-tuple-element.2), calls=%async_computation.2 | async-start | bytes 1572864 | tf_op jit(solution)/shard_map/all_to_all | solution.py:72
  101.1 18.7 %all-gather.6.cloned.1.call-done = bf16[320,2048]{1,0:T(8,128)(2,1)} async-done(((bf16[320,1024]{1,0:T(8,128)(2,1)}), bf16[320,2048]{1,0:T(8,128)(2,1)}) %all-gather.6.cloned.1.call-update) | async-done | bytes 1310736 | tf_op jit(solution)/shard_map/all_gather | solution.py:75
  119.8 3.6 %fusion.5 = f32[320,704]{1,0:T(8,128)S(1)} fusion(bf16[320,2048]{1,0:T(8,128)(2,1)} %all-gather.6.cloned.1.call-done, bf16[1,2048,704]{1,2,0:T(8,128)(2,1)} %param.16), kind=kOutput, calls=%fused_computation.10 | convolution fusion | flops 922746880 | bytes 5095424 | tf_op jit(solution)/shard_map/dot_general | solution.py:77
  123.4 1.3 fusion.16
  124.7 12.9 %all-gather = bf16[2,704,320]{1,2,0:T(8,128)(2,1)S(1)} all-gather(bf16[1,704,320]{1,2,0:T(8,128)(2,1)S(1)} %fusion.16), channel_id=1, replica_groups=mesh['dp'=2,'expert'=16] {'dp'}, dimensions={0}, use_global_device_ids=true | all-gather | bytes 1351680 | tf_op jit(solution)/shard_map/all_gather | solution.py:81
  137.6 2.0 %copy.20 = bf16[2,704,320]{1,0,2:T(2,128)(2,1)} copy(bf16[2,704,320]{1,2,0:T(8,128)(2,1)S(1)} %all-gather) | data formatting | bytes 1802240 | tf_op jit(solution)/shard_map/all_gather | solution.py:81
  139.6 3.4 %reshape.96 = bf16[1408,320]{0,1:T(8,128)(2,1)} reshape(bf16[2,704,320]{1,0,2:T(2,128)(2,1)} %copy.20) | data formatting | bytes 1802240
  143.0 2.4 %fusion.10 = bf16[320,1024]{1,0:T(8,128)(2,1)S(1)} fusion(bf16[1408,320]{0,1:T(8,128)(2,1)} %reshape.96, bf16[1,1408,1024]{2,1,0:T(8,128)(2,1)S(1)} %copy-done), kind=kOutput, calls=%fused_computation.14 | convolution fusion | flops 923074560 | bytes 4440064 | tf_op jit(solution)/shard_map/dot_general | solution.py:82
  145.4 1.0 reshape.58
  146.4 7.2 %all-to-all-start.1 = ((bf16[16,20,1024]{2,1,0:T(8,128)(2,1)}), bf16[16,20,1024]{2,1,0:T(8,128)(2,1)}, u32[]{:S(2)}, u32[]{:S(2)}) async-start(bf16[16,20,1024]{2,1,0:T(8,128)(2,1)} %reshape.58), calls=%async_computation.1 | async-start | bytes 1572864 | tf_op jit(solution)/shard_map/all_to_all | solution.py:89
  153.7 1.3 reshape.60
  154.9 4.4 %fusion = bf16[1,1408,1024]{2,1,0:T(8,128)(2,1)} fusion(bf16[1408,320]{0,1:T(8,128)(2,1)} %reshape.96, bf16[320,1024]{1,0:T(8,128)(2,1)S(1)} %reshape.60), kind=kOutput, calls=%fused_computation.5 | convolution fusion | flops 924188672 | bytes 4440064 | tf_op jit(solution)/shard_map/dot_general | solution.py:83
  159.4 13.9 %all-to-all-done.1 = bf16[16,20,1024]{2,1,0:T(8,128)(2,1)} async-done(((bf16[16,20,1024]{2,1,0:T(8,128)(2,1)}), bf16[16,20,1024]{2,1,0:T(8,128)(2,1)}, u32[]{:S(2)}, u32[]{:S(2)}) %all-to-all-start.1) | async-done | bytes 655392 | tf_op jit(solution)/shard_map/all_to_all | solution.py:89
  173.3 1.2 reshape.59
  174.6 2.0 %gather_fusion.1 = bf16[256,1024]{1,0:T(8,128)(2,1)} fusion(bf16[320,1024]{1,0:T(8,128)(2,1)S(1)} %reshape.59, s32[1024]{0:T(1024)S(1)} %pad_clamp_fusion), kind=kCustom, calls=%fused_computation.1 | custom fusion | bytes 1049600 | tf_op jit(solution)/shard_map/gather | solution.py:91
  176.6 2.0 %multiply_convert_fusion.1 = bf16[256,1024]{1,0:T(8,128)(2,1)} fusion(bf16[256,1024]{1,0:T(8,128)(2,1)} %gather_fusion.1, f32[256]{0:T(256)S(1)} %bitcast.60), kind=kLoop, calls=%fused_computation.24 | loop fusion | flops 786432 | bytes 1049600 | tf_op jit(solution)/shard_map/convert_element_type | solution.py:91
  (34 shorter events, 3.0 us)
Async XLA Ops:
  7.2 135.9 %copy-start = (bf16[1,1408,1024]{2,1,0:T(8,128)(2,1)S(1)}, bf16[1,1408,1024]{2,1,0:T(8,128)(2,1)}, u32[]{:S(2)}) copy-start(bf16[1,1408,1024]{2,1,0:T(8,128)(2,1)} %param.18) | copy-start | bytes 8650756
  7.2 13.0 %copy-start.1 = (s32[256,1]{0,1:T(1,128)S(1)}, s32[256,1]{0,1:T(1,128)}, u32[]{:S(2)}) copy-start(s32[256,1]{0,1:T(1,128)} %param.12) | copy-start | bytes 3076
  7.2 15.3 %copy-start.2 = (f32[256,1]{0,1:T(1,128)S(1)}, f32[256,1]{0,1:T(1,128)}, u32[]{:S(2)}) copy-start(f32[256,1]{0,1:T(1,128)} %param.13) | copy-start | bytes 3076
  7.2 46.4 %all-gather.4.cloned.1.call-start = ((), (), s32[]{:S(2)}) async-start(), calls=%async_computation.3 | async-start | bytes 2506752 | tf_op jit(solution)/shard_map/all_gather | solution.py:44
  7.9 111.9 %all-gather.6.cloned.1.call-start = ((), (), s32[]{:S(2)}) async-start(), calls=%async_computation.4 | async-start | bytes 1966080 | tf_op jit(solution)/shard_map/all_gather | solution.py:75
  28.5 32.4 %dynamic-slice-start = ((f32[2048]{0:T(1024)}, s32[]{:T(128)}), f32[1024]{0:T(1024)S(1)}, s32[]{:S(2)}) async-start(f32[2048]{0:T(1024)} %param.15, s32[]{:T(128)} %select_n.20), calls=%async_computation.5 | async-start | bytes 8704 | tf_op jit(solution)/shard_map/dynamic_slice | solution.py:47
  96.6 49.8 %all-to-all-start.2 = ((bf16[16,20,1024]{2,1,0:T(8,128)(2,1)}), bf16[16,20,1024]{2,1,0:T(8,128)(2,1)}, u32[]{:S(2)}, u32[]{:S(2)}) async-start(bf16[16,20,1024]{2,1,0:T(8,128)(2,1)} %get-tuple-element.2), calls=%async_computation.2 | async-start | bytes 1572864 | tf_op jit(solution)/shard_map/all_to_all | solution.py:72
  119.8 3.6 %copy-start.3 = (bf16[1,2048,704]{1,2,0:T(8,128)(2,1)S(1)}, bf16[1,2048,704]{1,2,0:T(8,128)(2,1)}, u32[]{:S(2)}) copy-start(bf16[1,2048,704]{1,2,0:T(8,128)(2,1)} %param.17) | copy-start | bytes 8650756
  119.8 3.6 %copy-start.4 = (bf16[320,2048]{1,0:T(8,128)(2,1)S(1)}, bf16[320,2048]{1,0:T(8,128)(2,1)}, u32[]{:S(2)}) copy-start(bf16[320,2048]{1,0:T(8,128)(2,1)} %all-gather.6.cloned.1.call-done) | copy-start | bytes 3932164
  146.4 26.9 %all-to-all-start.1 = ((bf16[16,20,1024]{2,1,0:T(8,128)(2,1)}), bf16[16,20,1024]{2,1,0:T(8,128)(2,1)}, u32[]{:S(2)}, u32[]{:S(2)}) async-start(bf16[16,20,1024]{2,1,0:T(8,128)(2,1)} %reshape.58), calls=%async_computation.1 | async-start | bytes 1572864 | tf_op jit(solution)/shard_map/all_to_all | solution.py:89
Sparse Core Ops, SparseCore 0:
  10.3 43.2 all-gather.3
  96.7 23.0 all-gather.5
where the time goes:
time: 186 us; the launch traced here: 185 us
  waiting for transfers between devices  58.5 us (31%)
  blocking collectives  50.8 us (27%)
  local copies, waits for them, and re-layouts  25.4 us (14%)
  matrix products  15.8 us (8%)
  between operations  14.2 us (8%)
  starting transfers between devices  11.8 us (6%)
  other arithmetic  8.93 us (5%)
    all_to_all x1, blocking collectives, body(): lax.all_to_all(arrange(source_rows), 'expert', split_axis=0, concat_axis=...  25.4 us
    all_gather x1, waiting for transfers between devices, body(): lax.all_gather(proj_weight, 'expert', axis=0, tiled=True)  25.1 us
    all_gather x1, waiting for transfers between devices, body(): lax.all_gather(sent_rows.reshape(slot_count, slice_width), 'dp', axis=1,...  18.7 us
    all_to_all x1, waiting for transfers between devices, body(): lax.all_to_all(expert_out, 'expert', split_axis=0, concat_axis=0, tiled=T...  13.9 us
    all_gather x1, blocking collectives, body(): shard_piece = lax.all_gather(hidden, 'dp', axis=1, tiled=True)  12.9 us
    gather x4, local copies, waits for them, and re-layouts, arrange(): row_block[source_row]  9.29 us
    all_gather x1, blocking collectives, body(): shard_piece = lax.all_gather(cache, 'dp', axis=0, tiled=True)  8.75 us
    all_to_all x1, starting transfers between devices, body(): lax.all_to_all(expert_out, 'expert', split_axis=0, concat_axis=0, tiled=T...  7.25 us
  transfers between devices with their start and end apart: 4, of which 3 were waited for; matrix products, arithmetic and copies ran while one was open for 17% of the time, Pallas kernels for 0%

commit v1 on v0

--- a/solution.py
+++ b/solution.py
@@ -2,6 +2,7 @@
 import jax.numpy as jnp
 from jax import lax
 from jax.sharding import PartitionSpec as P
+from jax.lax import all_gather
 
 
 def normalize(row_block, gain_row, sum_squares, model_width):
@@ -45,7 +46,9 @@
         preferred_element_type=jnp.float32,
     ).astype(jnp.bfloat16)
     gain_slice = lax.dynamic_slice_in_dim(norm_gain, dp_rank * slice_width, slice_width)
-    sum_squares = lax.psum(local_squares(projected), "dp")
+    sample = local_squares(projected)
+    carry = all_gather(sample, "dp")
+    sum_squares = jnp.sum(carry, axis=0)
     source_rows = normalize(projected, gain_slice, sum_squares, model_width)
     experts = lax.axis_size("expert") * gate_weight.shape[0]
     capacity = max(2, 5 * tokens // (4 * experts))

time: 186 us -> 186 us (level)
    psum x1 -> x0, blocking collectives: 3.77 us -> none  [body(): sum_squares = lax.psum(local_squares(projected), 'dp')]
    all_gather x0 -> x1, blocking collectives: none -> 3.08 us  [body(): carry = all_gather(sample, 'dp')]
where the time goes in v1:
time: 186 us; the launch traced here: 185 us
  waiting for transfers between devices  58.5 us (31%)
  blocking collectives  50.1 us (27%)
  local copies, waits for them, and re-layouts  25.4 us (14%)
  matrix products  15.8 us (8%)
  between operations  14.2 us (8%)
  starting transfers between devices  11.8 us (6%)
  other arithmetic  8.95 us (5%)
    all_to_all x1, blocking collectives, body(): lax.all_to_all(arrange(source_rows), 'expert', split_axis=0, concat_axis=...  25.4 us
    all_gather x1, waiting for transfers between devices, body(): lax.all_gather(proj_weight, 'expert', axis=0, tiled=True)  25.1 us
    all_gather x1, waiting for transfers between devices, body(): lax.all_gather(sent_rows.reshape(slot_count, slice_width), 'dp', axis=1,...  18.7 us
    all_to_all x1, waiting for transfers between devices, body(): lax.all_to_all(expert_out, 'expert', split_axis=0, concat_axis=0, tiled=T...  13.9 us
    all_gather x1, blocking collectives, body(): shard_piece = lax.all_gather(hidden, 'dp', axis=1, tiled=True)  12.9 us
    gather x4, local copies, waits for them, and re-layouts, arrange(): row_block[source_row]  9.29 us
    all_gather x1, blocking collectives, body(): shard_piece = lax.all_gather(cache, 'dp', axis=0, tiled=True)  8.75 us
    all_to_all x1, starting transfers between devices, body(): lax.all_to_all(expert_out, 'expert', split_axis=0, concat_axis=0, tiled=T...  7.26 us
  transfers between devices with their start and end apart: 4, of which 3 were waited for; matrix products, arithmetic and copies ran while one was open for 17% of the time, Pallas kernels for 0%

profile of v1, /device:TPU:9, one launch (start us, length us, event | category | flops | bytes accessed | tf_op | source)
XLA Modules:
  0.0 184.7 jit_solution(11517015578774489140)
XLA Ops:
  8.5 1.3 reduce.6
  9.9 8.8 %all_gather.18 = bf16[4,64,1152]{2,1,0:T(8,128)(2,1)S(1)} all-gather(bf16[2,64,1152]{2,1,0:T(8,128)(2,1)} %param.10), channel_id=1, replica_groups=mesh['dp'=2,'expert'=16] {'dp'}, dimensions={0}, use_global_device_ids=true | all-gather | bytes 884736 | tf_op jit(solution)/shard_map/all_gather | solution.py:37
  19.3 0.9 copy.19
  21.1 1.4 scatter_custom_fusion
  22.5 1.2 multiply_convert_fusion
  23.7 2.6 %gather_fusion.2 = bf16[320,1024]{1,0:T(8,128)(2,1)} fusion(bf16[256,1024]{1,0:T(8,128)(2,1)S(1)} %multiply_convert_fusion, s32[1024]{0:T(1024)S(1)} %pad_clamp_fusion.1), kind=kCustom, calls=%fused_computation.2 | custom fusion | bytes 1312000 | tf_op jit(solution)/shard_map/gather | solution.py:68
  26.4 2.0 %gather.17 = bf16[16,20,1024]{2,1,0:T(8,128)(2,1)} reshape(bf16[320,1024]{1,0:T(8,128)(2,1)} %gather_fusion.2) | data formatting | bytes 1310720 | tf_op jit(solution)/shard_map/gather | solution.py:68
  28.5 25.1 %all-gather.6.cloned.1.call-done = bf16[1152,1024]{1,0:T(8,128)(2,1)} async-done(((bf16[72,1024]{1,0:T(8,128)(2,1)}), bf16[1152,1024]{1,0:T(8,128)(2,1)}) %all-gather.6.cloned.1.call-update) | async-done | bytes 2359312 | tf_op jit(solution)/shard_map/all_gather | solution.py:45
  53.6 3.5 %fusion.19 = (f32[256]{0:T(256)S(1)}, bf16[256,1024]{1,0:T(8,128)(2,1)}) fusion(bf16[256,1152]{1,0:T(8,128)(2,1)} %bitcast.57, bf16[1152,1024]{1,0:T(8,128)(2,1)} %all-gather.6.cloned.1.call-done), kind=kOutput, calls=%fused_computation.20 | convolution fusion | flops 605028096 | bytes 3474432 | tf_op jit(solution)/shard_map/dot_general | solution.py:43
  57.1 3.1 %all-gather.1 = f32[2,1,256]{2,1,0:T(1,128)S(1)} all-gather(f32[1,1,256]{2,1,0:T(1,128)S(1)} %bitcast.65), channel_id=2, replica_groups=mesh['dp'=2,'expert'=16] {'dp'}, dimensions={0}, use_global_device_ids=true | all-gather | bytes 3072 | tf_op jit(solution)/shard_map/all_gather | solution.py:50
  60.2 1.2 fusion.21
  61.5 2.6 %gather_fusion = bf16[320,1024]{1,0:T(8,128)(2,1)} fusion(bf16[256,1024]{1,0:T(8,128)(2,1)S(1)} %fusion.21, s32[1024]{0:T(1024)S(1)} %pad_clamp_fusion.1), kind=kCustom, calls=%fused_computation | custom fusion | bytes 1312000 | tf_op jit(solution)/shard_map/gather | solution.py:68
  64.1 2.0 %gather.14 = bf16[16,20,1024]{2,1,0:T(8,128)(2,1)} reshape(bf16[320,1024]{1,0:T(8,128)(2,1)} %gather_fusion) | data formatting | bytes 1310720 | tf_op jit(solution)/shard_map/gather | solution.py:68
  66.1 2.4 %broadcast_select_fusion = (bf16[16,20,1024]{2,1,0:T(8,128)(2,1)}, bf16[16,20,1024]{2,1,0:T(8,128)(2,1)S(1)}) fusion(bf16[16,20,1024]{2,1,0:T(8,128)(2,1)} %gather.17, pred[16,20]{1,0:T(8,128)(4,1)S(1)} %broadcast_in_dim.33, bf16[16,20,1024]{2,1,0:T(8,128)(2,1)} %gather.14), kind=kLoop, calls=%fused_computation.25 | loop fusion | flops 655360 | bytes 2621760 | tf_op jit(solution)/shard_map/jit(_where)/select_n | solution.py:68
  68.5 25.4 %all_to_all.15 = bf16[16,20,1024]{2,1,0:T(8,128)(2,1)} all-to-all(bf16[16,20,1024]{2,1,0:T(8,128)(2,1)S(1)} %get-tuple-element.3), channel_id=1, replica_groups=mesh['dp'=2,'expert'=16] {'expert'}, dimensions={0} | all-to-all | bytes 1310720 | tf_op jit(solution)/shard_map/all_to_all | solution.py:74
  93.9 2.0 %reshape.61 = bf16[320,1024]{1,0:T(8,128)(2,1)} reshape(bf16[16,20,1024]{2,1,0:T(8,128)(2,1)} %all_to_all.15) | data formatting | bytes 1310720 | tf_op jit(solution)/shard_map/reshape | solution.py:78
  95.9 4.5 %all-to-all-start.2 = ((bf16[16,20,1024]{2,1,0:T(8,128)(2,1)}), bf16[16,20,1024]{2,1,0:T(8,128)(2,1)}, u32[]{:S(2)}, u32[]{:S(2)}) async-start(bf16[16,20,1024]{2,1,0:T(8,128)(2,1)} %get-tuple-element.2), calls=%async_computation.2 | async-start | bytes 1572864 | tf_op jit(solution)/shard_map/all_to_all | solution.py:75
  100.4 18.7 %all-gather.8.cloned.1.call-done = bf16[320,2048]{1,0:T(8,128)(2,1)} async-done(((bf16[320,1024]{1,0:T(8,128)(2,1)}), bf16[320,2048]{1,0:T(8,128)(2,1)}) %all-gather.8.cloned.1.call-update) | async-done | bytes 1310736 | tf_op jit(solution)/shard_map/all_gather | solution.py:78
  119.1 3.6 %fusion.5 = f32[320,704]{1,0:T(8,128)S(1)} fusion(bf16[320,2048]{1,0:T(8,128)(2,1)} %all-gather.8.cloned.1.call-done, bf16[1,2048,704]{1,2,0:T(8,128)(2,1)} %param.16), kind=kOutput, calls=%fused_computation.10 | convolution fusion | flops 922746880 | bytes 5095424 | tf_op jit(solution)/shard_map/dot_general | solution.py:80
  122.7 1.3 fusion.16
  124.0 12.9 %all-gather.2 = bf16[2,704,320]{1,2,0:T(8,128)(2,1)S(1)} all-gather(bf16[1,704,320]{1,2,0:T(8,128)(2,1)S(1)} %fusion.16), channel_id=1, replica_groups=mesh['dp'=2,'expert'=16] {'dp'}, dimensions={0}, use_global_device_ids=true | all-gather | bytes 1351680 | tf_op jit(solution)/shard_map/all_gather | solution.py:84
  137.0 2.0 %copy.20 = bf16[2,704,320]{1,0,2:T(2,128)(2,1)} copy(bf16[2,704,320]{1,2,0:T(8,128)(2,1)S(1)} %all-gather.2) | data formatting | bytes 1802240 | tf_op jit(solution)/shard_map/all_gather | solution.py:84
  138.9 3.4 %reshape.103 = bf16[1408,320]{0,1:T(8,128)(2,1)} reshape(bf16[2,704,320]{1,0,2:T(2,128)(2,1)} %copy.20) | data formatting | bytes 1802240
  142.4 2.4 %fusion.10 = bf16[320,1024]{1,0:T(8,128)(2,1)S(1)} fusion(bf16[1408,320]{0,1:T(8,128)(2,1)} %reshape.103, bf16[1,1408,1024]{2,1,0:T(8,128)(2,1)S(1)} %copy-done), kind=kOutput, calls=%fused_computation.14 | convolution fusion | flops 923074560 | bytes 4440064 | tf_op jit(solution)/shard_map/dot_general | solution.py:85
  144.7 1.0 reshape.62
  145.8 7.3 %all-to-all-start.1 = ((bf16[16,20,1024]{2,1,0:T(8,128)(2,1)}), bf16[16,20,1024]{2,1,0:T(8,128)(2,1)}, u32[]{:S(2)}, u32[]{:S(2)}) async-start(bf16[16,20,1024]{2,1,0:T(8,128)(2,1)} %reshape.62), calls=%async_computation.1 | async-start | bytes 1572864 | tf_op jit(solution)/shard_map/all_to_all | solution.py:92
  153.0 1.3 reshape.64
  154.3 4.4 %fusion = bf16[1,1408,1024]{2,1,0:T(8,128)(2,1)} fusion(bf16[1408,320]{0,1:T(8,128)(2,1)} %reshape.103, bf16[320,1024]{1,0:T(8,128)(2,1)S(1)} %reshape.64), kind=kOutput, calls=%fused_computation.5 | convolution fusion | flops 924188672 | bytes 4440064 | tf_op jit(solution)/shard_map/dot_general | solution.py:86
  158.7 13.9 %all-to-all-done.1 = bf16[16,20,1024]{2,1,0:T(8,128)(2,1)} async-done(((bf16[16,20,1024]{2,1,0:T(8,128)(2,1)}), bf16[16,20,1024]{2,1,0:T(8,128)(2,1)}, u32[]{:S(2)}, u32[]{:S(2)}) %all-to-all-start.1) | async-done | bytes 655392 | tf_op jit(solution)/shard_map/all_to_all | solution.py:92
  172.7 1.2 reshape.63
  173.9 2.0 %gather_fusion.1 = bf16[256,1024]{1,0:T(8,128)(2,1)} fusion(bf16[320,1024]{1,0:T(8,128)(2,1)S(1)} %reshape.63, s32[1024]{0:T(1024)S(1)} %pad_clamp_fusion), kind=kCustom, calls=%fused_computation.1 | custom fusion | bytes 1049600 | tf_op jit(solution)/shard_map/gather | solution.py:94
  175.9 2.0 %multiply_convert_fusion.1 = bf16[256,1024]{1,0:T(8,128)(2,1)} fusion(bf16[256,1024]{1,0:T(8,128)(2,1)} %gather_fusion.1, f32[256]{0:T(256)S(1)} %bitcast.61), kind=kLoop, calls=%fused_computation.24 | loop fusion | flops 786432 | bytes 1049600 | tf_op jit(solution)/shard_map/convert_element_type | solution.py:94
  (35 shorter events, 3.1 us)
Async XLA Ops:
  7.2 135.2 %copy-start = (bf16[1,1408,1024]{2,1,0:T(8,128)(2,1)S(1)}, bf16[1,1408,1024]{2,1,0:T(8,128)(2,1)}, u32[]{:S(2)}) copy-start(bf16[1,1408,1024]{2,1,0:T(8,128)(2,1)} %param.18) | copy-start | bytes 8650756
  7.2 13.0 %copy-start.1 = (s32[256,1]{0,1:T(1,128)S(1)}, s32[256,1]{0,1:T(1,128)}, u32[]{:S(2)}) copy-start(s32[256,1]{0,1:T(1,128)} %param.12) | copy-start | bytes 3076
  7.2 15.3 %copy-start.2 = (f32[256,1]{0,1:T(1,128)S(1)}, f32[256,1]{0,1:T(1,128)}, u32[]{:S(2)}) copy-start(f32[256,1]{0,1:T(1,128)} %param.13) | copy-start | bytes 3076
  7.2 46.4 %all-gather.6.cloned.1.call-start = ((), (), s32[]{:S(2)}) async-start(), calls=%async_computation.3 | async-start | bytes 2506752 | tf_op jit(solution)/shard_map/all_gather | solution.py:45
  7.9 111.2 %all-gather.8.cloned.1.call-start = ((), (), s32[]{:S(2)}) async-start(), calls=%async_computation.4 | async-start | bytes 1966080 | tf_op jit(solution)/shard_map/all_gather | solution.py:78
  28.5 31.8 %dynamic-slice-start = ((f32[2048]{0:T(1024)}, s32[]{:T(128)}), f32[1024]{0:T(1024)S(1)}, s32[]{:S(2)}) async-start(f32[2048]{0:T(1024)} %param.15, s32[]{:T(128)} %select_n.20), calls=%async_computation.5 | async-start | bytes 8704 | tf_op jit(solution)/shard_map/dynamic_slice | solution.py:48
  95.9 49.8 %all-to-all-start.2 = ((bf16[16,20,1024]{2,1,0:T(8,128)(2,1)}), bf16[16,20,1024]{2,1,0:T(8,128)(2,1)}, u32[]{:S(2)}, u32[]{:S(2)}) async-start(bf16[16,20,1024]{2,1,0:T(8,128)(2,1)} %get-tuple-element.2), calls=%async_computation.2 | async-start | bytes 1572864 | tf_op jit(solution)/shard_map/all_to_all | solution.py:75
  119.1 3.6 %copy-start.3 = (bf16[1,2048,704]{1,2,0:T(8,128)(2,1)S(1)}, bf16[1,2048,704]{1,2,0:T(8,128)(2,1)}, u32[]{:S(2)}) copy-start(bf16[1,2048,704]{1,2,0:T(8,128)(2,1)} %param.17) | copy-start | bytes 8650756
  119.1 3.6 %copy-start.4 = (bf16[320,2048]{1,0:T(8,128)(2,1)S(1)}, bf16[320,2048]{1,0:T(8,128)(2,1)}, u32[]{:S(2)}) copy-start(bf16[320,2048]{1,0:T(8,128)(2,1)} %all-gather.8.cloned.1.call-done) | copy-start | bytes 3932164
  145.8 26.9 %all-to-all-start.1 = ((bf16[16,20,1024]{2,1,0:T(8,128)(2,1)}), bf16[16,20,1024]{2,1,0:T(8,128)(2,1)}, u32[]{:S(2)}, u32[]{:S(2)}) async-start(bf16[16,20,1024]{2,1,0:T(8,128)(2,1)} %reshape.62), calls=%async_computation.1 | async-start | bytes 1572864 | tf_op jit(solution)/shard_map/all_to_all | solution.py:92
Sparse Core Ops, SparseCore 0:
  10.3 43.2 all-gather.5
  96.0 23.0 all-gather.7
